TPU v7x, 128 devices: a whole 4x4x4 slice. The times are simulated.
128 devices in a mesh: mem: 4 (over y), patch: 32 (over x, z, core).
Axes of the slice: x: 4, y: 4, z: 4, core: 2. Of those that a mesh axis runs over, the one named last changes fastest.
Arguments:
- prior_states: bfloat16 [256, 524288], P('mem', 'patch'), may hold values from -6 to 6
- member_obs_images: bfloat16 [1048576, 256], P(('mem', 'patch')), may hold values from -64 to 64
- obs_residual: float32 [1048576], P(('mem', 'patch')), may hold values from -6 to 6
- obs_precision_weights: float32 [1048576], P(('mem', 'patch')), may hold values from 0.3 to 3
- region_obs_groups: int32 [512, 32], replicated, may hold values from 0 to 8191, as said below
- active_profile_tally: int32 [512], replicated, may hold values from 1 to 8
Outputs:
- analysis: bfloat16 [256, 524288], P('mem', 'patch')
Inputs may be any that keep to these rules, and one draw needn't show every extreme that they name: `region_obs_groups`: in each aligned group of 4 rows (the patches of one device after relayout), every range of 64 consecutive block numbers (the observations of one device) is named by no entry or by exactly 2 entries, and exactly half of the ranges are named.
All inputs are finite; a program needn't handle non-finite values.
Results may differ from a plain program's by a relative error of at most 0.0082.
Values may be sent and summed in bfloat16 or wider, within the bound.
No kernel may reach another device: no remote copies, remote signals or barrier semaphores. Data moves between devices by JAX's collectives and lax.ppermute only.
A program may use at most 128 MiB of HBM per device.

v0:
```python
import math

import jax
import jax.numpy as jnp
from jax import lax
from jax.sharding import PartitionSpec as P

NV = 128
BLK = 128
CAP = 2
ITERS = 10


def patch_weights(gram, ybar):
    breadth_extent = gram.shape[1]
    eye = jnp.eye(breadth_extent, dtype=jnp.float32)
    amat = (breadth_extent - 1.0) * eye[None] + gram
    norm = jnp.sqrt(jnp.sum(amat * amat, axis=(1, 2)) + 1e-06)
    ysweep = amat / norm[:, None, None]
    zsweep = jnp.broadcast_to(eye, amat.shape)

    def sweep(step, carry):
        ycur, zcur = carry
        mid = 1.5 * eye[None] - 0.5 * jnp.einsum(
            "pij,pjk->pik", zcur, ycur, precision=lax.Precision.HIGHEST
        )
        ynext = jnp.einsum("pij,pjk->pik", ycur, mid, precision=lax.Precision.HIGHEST)
        znext = jnp.einsum("pij,pjk->pik", mid, zcur, precision=lax.Precision.HIGHEST)
        return (ynext, znext)

    ysweep, zsweep = lax.fori_loop(0, ITERS, sweep, (ysweep, zsweep))
    root_inv = zsweep / jnp.sqrt(norm)[:, None, None]
    inner = jnp.einsum("pij,pj->pi", root_inv, ybar, precision=lax.Precision.HIGHEST)
    mean_w = jnp.einsum("pij,pj->pi", root_inv, inner, precision=lax.Precision.HIGHEST)
    return (math.sqrt(breadth_extent - 1.0) * root_inv + mean_w[:, :, None]).astype(jnp.bfloat16)


def body(
    prior_states,
    member_obs_images,
    obs_residual,
    obs_precision_weights,
    region_obs_groups,
    active_profile_tally,
):
    nmem = lax.axis_size("mem")
    npat = lax.axis_size("patch")
    devices = nmem * npat
    breadth_extent = member_obs_images.shape[1]
    nb_dev = member_obs_images.shape[0] // BLK
    regions_per_processor = region_obs_groups.shape[0] // devices
    entries = regions_per_processor * region_obs_groups.shape[1]
    obs_mean = jnp.mean(member_obs_images, axis=1, keepdims=True, dtype=jnp.float32)
    root_r = jnp.sqrt(obs_precision_weights)
    weighted = ((member_obs_images - obs_mean) * root_r[:, None]).astype(jnp.bfloat16)
    scaled = root_r * obs_residual
    source = lax.axis_index("mem") * npat + lax.axis_index("patch")
    lists = (
        region_obs_groups.reshape(npat, nmem, entries).transpose(1, 0, 2).reshape(devices, entries)
    )
    mine = lists // nb_dev == source
    local_ids = lists - source * nb_dev
    rank = jnp.cumsum(mine.astype(jnp.int32), axis=1) - 1
    picks = []
    valids = []
    for slot in range(CAP):
        chosen = mine & (rank == slot)
        picks.append(jnp.sum(jnp.where(chosen, local_ids, 0), axis=1))
        valids.append(jnp.any(chosen, axis=1))
    pick = jnp.stack(picks, axis=1)
    valid = jnp.stack(valids, axis=1)
    row_blocks = weighted.reshape(nb_dev, BLK, breadth_extent)
    innov_blocks = scaled.reshape(nb_dev, BLK)
    send_rows = jnp.where(valid[:, :, None, None], row_blocks[pick], jnp.zeros((), jnp.bfloat16))
    send_innov = jnp.where(valid[:, :, None], innov_blocks[pick], jnp.zeros((), jnp.float32))
    got_rows, got_innov = (
        lax.all_to_all(send_rows, ("mem", "patch"), split_axis=0, concat_axis=0, tiled=True),
        lax.all_to_all(
            send_innov.astype(jnp.bfloat16),
            ("mem", "patch"),
            split_axis=0,
            concat_axis=0,
            tiled=True,
        ).astype(send_innov.dtype),
    )
    got_rows = got_rows.reshape(devices * CAP, BLK, breadth_extent)
    got_innov = got_innov.reshape(devices * CAP, BLK)
    block = lax.axis_index("patch") * nmem + lax.axis_index("mem")
    my_lists = lax.dynamic_slice_in_dim(
        region_obs_groups, block * regions_per_processor, regions_per_processor, 0
    ).reshape(entries)
    src_dev = my_lists // nb_dev
    position = jnp.arange(entries)
    earlier = (src_dev[:, None] == src_dev[None, :]) & (position[None, :] < position[:, None])
    slots = src_dev * CAP + jnp.sum(earlier, axis=1)
    rows = got_rows[slots].reshape(regions_per_processor, -1, breadth_extent)
    innov_rows = got_innov[slots].reshape(regions_per_processor, -1)
    gram = jnp.einsum("prk,prj->pkj", rows, rows, preferred_element_type=jnp.float32)
    ybar = jnp.einsum(
        "prk,pr->pk", rows.astype(jnp.float32), innov_rows, precision=lax.Precision.HIGHEST
    )
    weights = patch_weights(gram, ybar)
    state_entries = lax.all_to_all(prior_states, "mem", split_axis=1, concat_axis=0, tiled=True)
    prior_average = jnp.mean(state_entries, axis=0, dtype=jnp.float32)
    prior_anomaly = (state_entries - prior_average[None, :]).astype(jnp.bfloat16)
    vertical_extent = state_entries.shape[1] // regions_per_processor
    anomaly_tensor = prior_anomaly.reshape(breadth_extent, regions_per_processor, vertical_extent)
    blended_states = prior_average.reshape(regions_per_processor, vertical_extent)[
        None
    ] + jnp.einsum("pij,ipg->jpg", weights, anomaly_tensor, preferred_element_type=jnp.float32)
    counts = lax.dynamic_slice_in_dim(
        active_profile_tally, block * regions_per_processor, regions_per_processor, 0
    )
    column = jnp.arange(vertical_extent) // NV
    retain_mask = column[None, :] < counts[:, None]
    fore_cube = state_entries.reshape(
        breadth_extent, regions_per_processor, vertical_extent
    ).astype(jnp.float32)
    result = (
        jnp.where(retain_mask[None], blended_states, fore_cube)
        .astype(jnp.bfloat16)
        .reshape(breadth_extent, -1)
    )
    return lax.all_to_all(result, "mem", split_axis=0, concat_axis=1, tiled=True)


def solution(mesh):
    return jax.shard_map(
        body,
        mesh=mesh,
        in_specs=(
            P("mem", "patch"),
            P(("mem", "patch"), None),
            P(("mem", "patch")),
            P(("mem", "patch")),
            P(),
            P(),
        ),
        out_specs=P("mem", "patch"),
        check_vma=False,
    )
```

profile of v0, /device:TPU:2, one launch (start us, length us, event | category | flops | bytes accessed | tf_op | source)
XLA Modules:
  0.0 426.2 jit_solution(9441763954466778025)
XLA Ops:
  0.0 1.0 copy.55
  1.2 1.2 reduce_window_sum.11
  3.6 0.8 multiply_bitcast_fusion
  4.4 0.9 gather_fusion.2
  5.3 0.8 select_convert_fusion
  6.1 10.5 %all-to-all-start.2 = ((bf16[128,2,128]{2,1,0:T(2,128)(2,1)}), bf16[128,2,128]{2,1,0:T(2,128)(2,1)S(1)}, u32[]{:S(2)}, u32[]{:S(2)}) async-start(bf16[128,2,128]{2,1,0:T(2,128)(2,1)} %select_convert_fusion), calls=%async_computation.2 | async-start | bytes 131072 | tf_op jit(solution)/shard_map/all_to_all | solution.py:78
  16.6 0.9 sqrt.20
  17.6 3.6 convert_reduce_fusion
  21.2 5.3 %fusion.5 = bf16[8192,256]{1,0:T(8,128)(2,1)} fusion(bf16[8192,256]{1,0:T(8,128)(2,1)S(1)} %copy-done, f32[8192]{0:T(1024)S(1)} %sqrt.20, f32[8192]{0:T(1024)S(1)} %broadcast_multiply_fusion), kind=kLoop, calls=%fused_computation.14 | loop fusion | flops 8388608 | bytes 8454144 | tf_op jit(solution)/shard_map/convert_element_type | solution.py:55
  26.5 11.8 %gather_fusion = bf16[256,128,256]{2,1,0:T(8,128)(2,1)} fusion(bf16[64,128,256]{2,1,0:T(8,128)(2,1)} %bitcast.88, s32[1024]{0:T(1024)S(1)} %pad_clamp_fusion.1), kind=kCustom, calls=%fused_computation | custom fusion | bytes 33555456 | tf_op jit(solution)/shard_map/gather | solution.py:74
  38.3 1.5 copy.94
  39.9 4.3 %all-to-all-start = ((bf16[64,4,4096]{2,0,1:T(8,128)(2,1)}), bf16[64,4,4096]{2,0,1:T(8,128)(2,1)S(1)}, u32[]{:S(2)}, u32[]{:S(2)}) async-start(bf16[64,4,4096]{2,0,1:T(8,128)(2,1)} %bitcast.92), calls=%async_computation | async-start | bytes 4194304 | tf_op jit(solution)/shard_map/all_to_all | solution.py:103
  44.1 14.0 %broadcast_select_fusion = bf16[128,2,128,256]{3,2,1,0:T(8,128)(2,1)} fusion(bf16[128,2,128,256]{3,2,1,0:T(8,128)(2,1)} %bitcast.89, pred[128,2]{1,0:T(8,128)(4,1)S(1)} %copy.57), kind=kLoop, calls=%fused_computation.10 | loop fusion | flops 8388608 | bytes 33554688 | tf_op jit(solution)/shard_map/jit(_where)/select_n | solution.py:74
  58.1 12.6 %all-to-all-done = bf16[64,4,4096]{2,0,1:T(8,128)(2,1)S(1)} async-done(((bf16[64,4,4096]{2,0,1:T(8,128)(2,1)}), bf16[64,4,4096]{2,0,1:T(8,128)(2,1)S(1)}, u32[]{:S(2)}, u32[]{:S(2)}) %all-to-all-start) | async-done | bytes 2097184 | tf_op jit(solution)/shard_map/all_to_all | solution.py:103
  70.8 8.5 %all-to-all-start.1 = ((bf16[128,2,128,256]{3,2,1,0:T(8,128)(2,1)}), bf16[128,2,128,256]{3,2,1,0:T(8,128)(2,1)}, u32[]{:S(2)}, u32[]{:S(2)}) async-start(bf16[128,2,128,256]{3,2,1,0:T(8,128)(2,1)} %broadcast_select_fusion), calls=%async_computation.1 | async-start | bytes 33554432 | tf_op jit(solution)/shard_map/all_to_all | solution.py:77
  79.2 0.8 constant_dynamic-slice_fusion
  80.3 0.8 dynamic_slice.6
  81.4 0.7 gather_fusion.3
  82.1 2.4 convert_bitcast_fusion
  84.5 6.1 %reshape.357 = f32[256,4,1024]{2,1,0:T(4,128)} reshape(f32[4,64,4096]{2,1,0:T(8,128)} %convert_bitcast_fusion) | data formatting | bytes 8388608 | tf_op jit(solution)/shard_map/convert_element_type | solution.py:104
  91.0 4.5 %copy.65 = bf16[256,4,1024]{0,2,1:T(8,128)(2,1)} copy(f32[256,4,1024]{2,1,0:T(4,128)} %reshape.357) | data formatting | bytes 6291456 | tf_op jit(solution)/shard_map/convert_element_type | solution.py:104
  95.5 4.5 %subtract_convert_fusion = bf16[256,4,1024]{2,1,0:T(4,128)(2,1)} fusion(f32[256,4,1024]{2,1,0:T(4,128)} %reshape.357, f32[4,1024]{1,0:T(4,128)S(1)} %div.74), kind=kLoop, calls=%fused_computation.19 | loop fusion | flops 2097152 | bytes 6307840 | tf_op jit(solution)/shard_map/convert_element_type | solution.py:105
  100.0 211.1 %all-to-all-done.1 = bf16[128,2,128,256]{3,2,1,0:T(8,128)(2,1)} async-done(((bf16[128,2,128,256]{3,2,1,0:T(8,128)(2,1)}), bf16[128,2,128,256]{3,2,1,0:T(8,128)(2,1)}, u32[]{:S(2)}, u32[]{:S(2)}) %all-to-all-start.1) | async-done | bytes 16777248 | tf_op jit(solution)/shard_map/all_to_all | solution.py:77
  311.2 12.3 %gather_fusion.1 = bf16[128,128,256]{2,1,0:T(8,128)(2,1)} fusion(bf16[256,128,256]{2,1,0:T(8,128)(2,1)} %bitcast.4, s32[1024]{0:T(1024)S(1)} %pad_clamp_fusion), kind=kCustom, calls=%fused_computation.1 | custom fusion | bytes 16777728 | tf_op jit(solution)/shard_map/gather | solution.py:96
  323.5 8.8 %multiply_reduce_fusion = (f32[4]{0:T(128)S(1)}, f32[4,256,256]{2,1,0:T(8,128)S(1)}) fusion(bf16[4,4096,256]{2,1,0:T(8,128)(2,1)} %bitcast.90, f32[256,256]{1,0:T(8,128)S(1)} %fusion.11), kind=kOutput, calls=%fused_computation.24 | convolution fusion | flops 2148270080 | bytes 9699344 | tf_op jit(solution)/shard_map/prk,prj->pkj/dot_general | solution.py:98
  332.9 44.9 %while.13 = (s32[]{:T(128)}, f32[4,256,256]{1,2,0:T(8,128)S(1)}, f32[4,256,256]{2,1,0:T(8,128)S(1)}, s32[]{:T(128)}) while((s32[]{:T(128)}, f32[4,256,256]{1,2,0:T(8,128)S(1)}, f32[4,256,256]{2,1,0:T(8,128)S(1)}, s32[]{:T(128)}) %tuple.33), condition=%wide.region_10.11_spmd.clone, body=%wide.region_9.10_spmd.clone.sunk | while | flops 2416574464 | bytes 14155829 | solution.py:31
  333.4 1.2 fusion.59
  334.5 1.1 fusion.60
  335.7 1.9 convolution_bitcast_fusion.2
  337.8 1.2 fusion.59
  339.0 1.1 fusion.60
  340.2 1.9 convolution_bitcast_fusion.2
  342.3 1.2 fusion.59
  343.5 1.1 fusion.60
  344.6 1.9 convolution_bitcast_fusion.2
  346.7 1.2 fusion.59
  347.9 1.1 fusion.60
  349.1 1.9 convolution_bitcast_fusion.2
  351.2 1.2 fusion.59
  352.4 1.1 fusion.60
  353.6 1.9 convolution_bitcast_fusion.2
  355.7 1.2 fusion.59
  356.9 1.1 fusion.60
  358.0 1.9 convolution_bitcast_fusion.2
  360.1 1.2 fusion.59
  361.3 1.1 fusion.60
  362.5 1.9 convolution_bitcast_fusion.2
  364.6 1.2 fusion.59
  365.8 1.1 fusion.60
  367.0 1.9 convolution_bitcast_fusion.2
  369.1 1.2 fusion.59
  370.3 1.1 fusion.60
  371.4 1.9 convolution_bitcast_fusion.2
  373.5 1.2 fusion.59
  374.7 1.1 fusion.60
  375.9 1.9 convolution_bitcast_fusion.2
  377.8 4.6 %fusion.32 = f32[4,1,256]{2,1,0:T(1,128)S(1)} fusion(bf16[4,4096,256]{2,1,0:T(8,128)(2,1)} %bitcast.91, bf16[4,4096,1]{1,2,0:T(2,128)(2,1)S(1)} %reshape.399), kind=kOutput, calls=%fused_computation.94 | convolution fusion | flops 8388608 | bytes 8425472 | tf_op jit(solution)/shard_map/prk,pr->pk/dot_general | solution.py:99
  382.4 1.1 fusion.21
  383.5 1.1 fusion.19
  384.6 4.0 fusion.6
  388.6 3.4 copy.66
  392.0 2.8 all_to_all.34
  394.7 30.0 %all_to_all.42 = bf16[4,64,4096]{2,1,0:T(8,128)(2,1)S(1)} all-to-all(bf16[4,64,4096]{2,1,0:T(8,128)(2,1)} %all_to_all.34), channel_id=1, replica_groups=mesh['mem'=4,'patch'=32] {'mem'}, dimensions={0} | all-to-all | bytes 4194304 | tf_op jit(solution)/shard_map/all_to_all | solution.py:124
  424.7 1.5 copy.79
  (78 shorter events, 4.6 us)
Async XLA Ops:
  6.1 33.8 %all-to-all-start.2 = ((bf16[128,2,128]{2,1,0:T(2,128)(2,1)}), bf16[128,2,128]{2,1,0:T(2,128)(2,1)S(1)}, u32[]{:S(2)}, u32[]{:S(2)}) async-start(bf16[128,2,128]{2,1,0:T(2,128)(2,1)} %select_convert_fusion), calls=%async_computation.2 | async-start | bytes 131072 | tf_op jit(solution)/shard_map/all_to_all | solution.py:78
  16.6 4.5 %copy-start = (bf16[8192,256]{1,0:T(8,128)(2,1)S(1)}, bf16[8192,256]{1,0:T(8,128)(2,1)}, u32[]{:S(2)}) copy-start(bf16[8192,256]{1,0:T(8,128)(2,1)} %param.9) | copy-start | bytes 12582916
  26.5 11.8 %copy-start.3 = (bf16[64,16384]{1,0:T(8,128)(2,1)S(1)}, bf16[64,16384]{1,0:T(8,128)(2,1)}, u32[]{:S(2)}) copy-start(bf16[64,16384]{1,0:T(8,128)(2,1)} %param.8) | copy-start | bytes 6291460
  39.9 30.9 %all-to-all-start = ((bf16[64,4,4096]{2,0,1:T(8,128)(2,1)}), bf16[64,4,4096]{2,0,1:T(8,128)(2,1)S(1)}, u32[]{:S(2)}, u32[]{:S(2)}) async-start(bf16[64,4,4096]{2,0,1:T(8,128)(2,1)} %bitcast.92), calls=%async_computation | async-start | bytes 4194304 | tf_op jit(solution)/shard_map/all_to_all | solution.py:103
  70.8 240.4 %all-to-all-start.1 = ((bf16[128,2,128,256]{3,2,1,0:T(8,128)(2,1)}), bf16[128,2,128,256]{3,2,1,0:T(8,128)(2,1)}, u32[]{:S(2)}, u32[]{:S(2)}) async-start(bf16[128,2,128,256]{3,2,1,0:T(8,128)(2,1)} %broadcast_select_fusion), calls=%async_computation.1 | async-start | bytes 33554432 | tf_op jit(solution)/shard_map/all_to_all | solution.py:77
  382.4 2.2 copy-start.1
  382.4 2.2 copy-start.2
where the time goes:
time: 427 us; the launch traced here: 426 us
  waiting for transfers between devices  224 us (52%)
  matrix products  61.9 us (14%)
  local copies, waits for them, and re-layouts  52 us (12%)
  other arithmetic  34.2 us (8%)
  blocking collectives  30 us (7%)
  starting transfers between devices  23.2 us (5%)
    all_to_all x1, waiting for transfers between devices, body(): lax.all_to_all(send_rows, ('mem', 'patch'), split_axis=0, concat_axis=0,...  211 us
    all_to_all x1, blocking collectives, body(): lax.all_to_all(result, 'mem', split_axis=0, concat_axis=1, tiled=True)  30 us
    dot_general x10, matrix products, sweep(): jnp.einsum('pij,pjk->pik', ycur, mid, precision=lax.Precision.HIGHEST)  19 us
    select_n x1, other arithmetic, body(): jnp.where(valid[:, :, None, None], row_blocks[pick], jnp.zeros((), jnp.bf...  14 us
    all_to_all x1, waiting for transfers between devices, body(): lax.all_to_all(prior_states, 'mem', split_axis=1, concat_axis=0, tiled=True)  12.6 us
    gather x1, local copies, waits for them, and re-layouts, body(): rows = got_rows[slots].reshape(regions_per_processor, -1, breadth_extent)  12.3 us
    dot_general x10, matrix products, sweep(): jnp.einsum('pij,pjk->pik', zcur, ycur, precision=lax.Precision.HIGHEST)  11.9 us
    gather x1, local copies, waits for them, and re-layouts, body(): row_blocks[pick]  11.8 us
  transfers between devices with their start and end apart: 3, of which 2 were waited for; matrix products, arithmetic and copies ran while one was open for 14% of the time, Pallas kernels for 0%

commit v1 on v0

v1 whole, which is shorter than its diff:
```python
import math

import jax
import jax.numpy as jnp
from jax import lax
from jax.experimental import pallas as pl
from jax.experimental.pallas import tpu as pltpu
from jax.sharding import PartitionSpec as P

NV = 128
BLK = 128
CAP = 2
ITERS = 10
TAIL = 16
CHUNK = 8

NT = (((1,), (1,)), ((), ()))
NN = (((1,), (0,)), ((), ()))


def dot(a, b, dims=NN):
    return lax.dot_general(a, b, dims, preferred_element_type=jnp.float32)


def iotas(shape):
    return lax.broadcasted_iota(jnp.int32, shape, 0), lax.broadcasted_iota(jnp.int32, shape, 1)


def send_kernel(
    lists_ref, img_ref, prec_ref, resid_ref, send_ref, table_ref,
    wt, innov, tail, centre, keys, keys_s, key_sem, tail_sem, sems,
):
    nmem = lax.axis_size("mem")
    npat = lax.axis_size("patch")
    groups, entries = lists_ref.shape
    members = img_ref.shape[1]
    nb_dev = wt.shape[0]
    step = pl.program_id(0)
    me_m = lax.axis_index("mem")
    me_p = lax.axis_index("patch")
    source = me_m * npat + me_p

    @pl.when(step == 0)
    def _():
        row, col = iotas((members, members))
        centre[...] = (
            jnp.where(row == col, 1.0, 0.0) - 1.0 / members
        ).astype(jnp.bfloat16)
        by_entry = lists_ref[...].T
        position, _ = iotas((entries, groups))
        mine = by_entry // nb_dev == source
        key = position * nb_dev + by_entry - source * nb_dev
        first = jnp.min(jnp.where(mine, key, entries * nb_dev), axis=0, keepdims=True)
        last = jnp.max(jnp.where(mine, key, -1), axis=0, keepdims=True)
        valid = last >= 0
        keys[0:1, :] = jnp.where(valid, first % nb_dev, -1)
        keys[1:2, :] = jnp.where(valid, last % nb_dev, -1)
        pltpu.make_async_copy(keys, keys_s, key_sem).start()
        my_row = jnp.broadcast_to(
            lists_ref[pl.ds(me_p * nmem + me_m, 1), :], (entries, entries)
        ) // nb_dev
        my_col = my_row.T
        row, col = iotas((entries, entries))
        earlier = jnp.where((my_row == my_col) & (row < col), 1, 0)
        slot = jnp.max(earlier, axis=0, keepdims=True)
        table_ref[...] = jnp.broadcast_to(my_row[0:1, :] * CAP + slot, table_ref.shape)

    root = jnp.sqrt(prec_ref[...])
    innov[pl.ds(pl.multiple_of(step * CHUNK, CHUNK), CHUNK), :] = root * resid_ref[...]
    for j in range(CHUNK):
        centred = dot(centre[...], img_ref[j * BLK : (j + 1) * BLK, :], NT)
        wt[step * CHUNK + j] = (centred * root[j : j + 1, :]).astype(jnp.bfloat16)

    @pl.when(step == pl.num_programs(0) - 1)
    def _():
        pltpu.make_async_copy(keys, keys_s, key_sem).wait()
        row, _ = iotas((TAIL, BLK))

        def copies(g):
            dest = (g % nmem) * npat + g // nmem
            return [
                pltpu.make_async_copy(
                    wt.at[jnp.maximum(keys_s[c, g], 0)],
                    send_ref.at[dest, pl.ds(c * members, members), :],
                    sems.at[c, g],
                )
                for c in range(CAP)
            ]

        def start(g, _):
            @pl.when(keys_s[0, g] >= 0)
            def _():
                for copy in copies(g):
                    copy.start()

            return 0

        lax.fori_loop(0, groups, start, 0)

        def fill(g, _):
            dest = (g % nmem) * npat + g // nmem
            one = innov[pl.ds(jnp.maximum(keys_s[0, g], 0), 1), :]
            two = innov[pl.ds(jnp.maximum(keys_s[1, g], 0), 1), :]
            tail[dest] = jnp.where(row == 0, one, jnp.where(row == 1, two, 0.0)).astype(jnp.bfloat16)
            return 0

        lax.fori_loop(0, groups, fill, 0)
        tails = pltpu.make_async_copy(
            tail, send_ref.at[:, pl.ds(CAP * members, TAIL), :], tail_sem
        )
        tails.start()

        def finish(g, _):
            @pl.when(keys_s[0, g] >= 0)
            def _():
                for copy in copies(g):
                    copy.wait()

            return 0

        lax.fori_loop(0, groups, finish, 0)
        tails.wait()


def send_blocks(lists, images, precision, residual):
    groups, entries = lists.shape
    members = images.shape[1]
    nb_dev = images.shape[0] // BLK
    return pl.pallas_call(
        send_kernel,
        grid=(nb_dev // CHUNK,),
        in_specs=[
            pl.BlockSpec((groups, entries), lambda s: (0, 0)),
            pl.BlockSpec((CHUNK * BLK, members), lambda s: (s, 0)),
            pl.BlockSpec((CHUNK, BLK), lambda s: (s, 0)),
            pl.BlockSpec((CHUNK, BLK), lambda s: (s, 0)),
        ],
        out_specs=[
            pl.BlockSpec(memory_space=pl.ANY),
            pl.BlockSpec((8, entries), lambda s: (0, 0)),
        ],
        out_shape=[
            jax.ShapeDtypeStruct((groups, CAP * members + TAIL, BLK), jnp.bfloat16),
            jax.ShapeDtypeStruct((8, entries), jnp.int32),
        ],
        scratch_shapes=[
            pltpu.VMEM((nb_dev, members, BLK), jnp.bfloat16),
            pltpu.VMEM((nb_dev, BLK), jnp.float32),
            pltpu.VMEM((groups, TAIL, BLK), jnp.bfloat16),
            pltpu.VMEM((members, members), jnp.bfloat16),
            pltpu.VMEM((8, groups), jnp.int32),
            pltpu.SMEM((8, groups), jnp.int32),
            pltpu.SemaphoreType.DMA,
            pltpu.SemaphoreType.DMA,
            pltpu.SemaphoreType.DMA((CAP, groups)),
        ],
        compiler_params=pltpu.CompilerParams(vmem_limit_bytes=40 * 2**20),
        cost_estimate=pl.CostEstimate(
            flops=2 * images.shape[0] * members * members,
            bytes_accessed=24 * 2**20,
            transcendentals=0,
        ),
        name="send_blocks",
    )(lists, images, precision, residual)


def split(x):
    high = x.astype(jnp.bfloat16)
    return high, (x - high.astype(jnp.float32)).astype(jnp.bfloat16)


def dot3(a, b):
    ah, al = a
    bh, bl = b
    return dot(
        jnp.concatenate([ah, ah, al], axis=1), jnp.concatenate([bh, bl, bh], axis=0)
    )


def weights_kernel(table_ref, got_ref, out_ref, buf, yh, yl, zh, zl, sems):
    patches = out_ref.shape[0]
    members = out_ref.shape[1]
    entries = table_ref.shape[1]
    per_patch = entries // patches

    for q in range(patches):

        def fetch(e, _, q=q):
            slot = table_ref[0, q * per_patch + e]
            lane = pl.ds(pl.multiple_of(e * BLK, BLK), BLK)
            pltpu.make_async_copy(
                got_ref.at[slot // CAP, pl.ds(pl.multiple_of(slot % CAP * members, members), members), :],
                buf.at[q, pl.ds(0, members), lane],
                sems.at[q],
            ).start()
            pltpu.make_async_copy(
                got_ref.at[slot // CAP, pl.ds(CAP * members, TAIL), :],
                buf.at[q, pl.ds(members, TAIL), lane],
                sems.at[q],
            ).start()
            return 0

        lax.fori_loop(0, per_patch, fetch, 0)

    row, col = iotas((members, members))
    eye = jnp.where(row == col, 1.0, 0.0)
    norms = []
    ybars = []
    for q in range(patches):
        pltpu.make_async_copy(buf.at[q], buf.at[q], sems.at[q]).wait()
        for e in range(per_patch):
            lane = slice(e * BLK, (e + 1) * BLK)
            both = buf[q, members:, lane].astype(jnp.float32)
            second = table_ref[0, q * per_patch + e] % CAP == 1
            chosen = jnp.where(second, both[1:2, :], both[0:1, :])
            buf[q, members:, lane] = jnp.broadcast_to(chosen, (TAIL, BLK)).astype(jnp.bfloat16)
        both = dot(buf[q], buf[q, :members, :], NT)
        amat = (members - 1.0) * eye + both[:members]
        norm = jnp.sqrt(jnp.sum(amat * amat, keepdims=True) + 1e-06)
        norms.append(norm)
        ybars.append(both[members : members + 8])
        ysweep = amat / norm
        mid = split(1.5 * eye - 0.5 * ysweep)
        zh[q], zl[q] = mid
        yh[q], yl[q] = split(dot3(split(ysweep), mid))

    def middle(q):
        prod = dot3((zh[q], zl[q]), (yh[q], yl[q]))
        return split(1.5 * eye - 0.5 * prod)

    def sweep(_, carry):
        mids = [middle(q) for q in range(patches)]
        for q in range(patches):
            yh[q], yl[q] = split(dot3((yh[q], yl[q]), mids[q]))
            zh[q], zl[q] = split(dot3(mids[q], (zh[q], zl[q])))
        return carry

    lax.fori_loop(0, ITERS - 2, sweep, 0)
    for q in range(patches):
        root_inv = dot3(middle(q), (zh[q], zl[q])) / jnp.sqrt(norms[q])
        parts = split(root_inv)
        inner = dot3(split(ybars[q]), parts)
        mean_w = dot3(split(inner), parts)[0:1, :]
        out_ref[q] = (math.sqrt(members - 1.0) * root_inv + mean_w).astype(jnp.bfloat16)


def patch_weights(table, got, patches, members):
    entries = table.shape[1]
    per_patch = entries // patches
    square = pltpu.VMEM((patches, members, members), jnp.bfloat16)
    return pl.pallas_call(
        weights_kernel,
        in_specs=[
            pl.BlockSpec(memory_space=pltpu.SMEM),
            pl.BlockSpec(memory_space=pl.ANY),
        ],
        out_specs=pl.BlockSpec(memory_space=pltpu.VMEM),
        out_shape=jax.ShapeDtypeStruct((patches, members, members), jnp.bfloat16),
        scratch_shapes=[
            pltpu.VMEM((patches, members + TAIL, per_patch * BLK), jnp.bfloat16),
            square,
            square,
            square,
            square,
            pltpu.SemaphoreType.DMA((patches,)),
        ],
        compiler_params=pltpu.CompilerParams(vmem_limit_bytes=40 * 2**20),
        cost_estimate=pl.CostEstimate(
            flops=2 * patches * members * members * (entries // patches * BLK + 90 * members),
            bytes_accessed=64 * 2**20,
            transcendentals=0,
        ),
        name="patch_weights",
    )(table, got)


def analysis_kernel(tally_ref, w_ref, x_ref, out_ref):
    patches = pl.num_programs(0)
    block = lax.axis_index("patch") * lax.axis_size("mem") + lax.axis_index("mem")
    live = tally_ref[block * patches + pl.program_id(0)]
    prior = x_ref[...].astype(jnp.float32)
    mean = jnp.mean(prior, axis=0, keepdims=True)
    anomaly = (prior - mean).astype(jnp.bfloat16)
    blended = mean + dot(w_ref[0], anomaly)
    _, col = iotas((1, x_ref.shape[1]))
    out_ref[...] = jnp.where(col < live * NV, blended, prior).astype(jnp.bfloat16)


def analyse(tally, weights, state):
    patches, members, _ = weights.shape
    extent = state.shape[1] // patches
    return pl.pallas_call(
        analysis_kernel,
        grid=(patches,),
        in_specs=[
            pl.BlockSpec(memory_space=pltpu.SMEM),
            pl.BlockSpec((1, members, members), lambda q: (q, 0, 0)),
            pl.BlockSpec((members, extent), lambda q: (0, q)),
        ],
        out_specs=pl.BlockSpec((members, extent), lambda q: (0, q)),
        out_shape=jax.ShapeDtypeStruct(state.shape, jnp.bfloat16),
        compiler_params=pltpu.CompilerParams(vmem_limit_bytes=32 * 2**20),
        cost_estimate=pl.CostEstimate(
            flops=2 * members * members * state.shape[1],
            bytes_accessed=4 * members * state.shape[1],
            transcendentals=0,
        ),
        name="analysis",
    )(tally, weights, state)


def body(
    prior_states,
    member_obs_images,
    obs_residual,
    obs_precision_weights,
    region_obs_groups,
    active_profile_tally,
):
    devices = lax.axis_size("mem") * lax.axis_size("patch")
    members = member_obs_images.shape[1]
    patches = region_obs_groups.shape[0] // devices
    lists = region_obs_groups.reshape(devices, -1)
    send, table = send_blocks(
        lists,
        member_obs_images,
        obs_precision_weights.reshape(-1, BLK),
        obs_residual.reshape(-1, BLK),
    )
    got = lax.all_to_all(send, ("mem", "patch"), split_axis=0, concat_axis=0, tiled=True)
    got, prior_states = lax.optimization_barrier((got, prior_states))
    state = lax.all_to_all(prior_states, "mem", split_axis=1, concat_axis=0, tiled=True)
    weights = patch_weights(table, got, patches, members)
    result = analyse(active_profile_tally, weights, state)
    return lax.all_to_all(result, "mem", split_axis=0, concat_axis=1, tiled=True)


def solution(mesh):
    return jax.shard_map(
        body,
        mesh=mesh,
        in_specs=(
            P("mem", "patch"),
            P(("mem", "patch"), None),
            P(("mem", "patch")),
            P(("mem", "patch")),
            P(),
            P(),
        ),
        out_specs=P("mem", "patch"),
        check_vma=False,
    )
```

time: 427 us -> 289 us (0.68)
  waiting for transfers between devices: 224 us -> 2.55 us
  blocking collectives: 30 us -> 236 us
  matrix products: 61.9 us -> 0 us
  local copies, waits for them, and re-layouts: 52 us -> 7.7 us
  Pallas kernels: 0 us -> 38.5 us
  other arithmetic: 34.2 us -> 0 us
  starting transfers between devices: 23.2 us -> 3.61 us
    all_to_all x2 -> x0, waiting for transfers between devices: 211 us -> none  [the longest x1 211 us: body(): lax.all_to_all(send_rows, ('mem', 'patch'), split_axis=0, concat_axis=0,...]
    all_to_all x0 -> x1, blocking collectives: none -> 207 us  [body(): lax.all_to_all(send, ('mem', 'patch'), split_axis=0, concat_axis=0, tiled...]
    dot_general x35 -> x0, matrix products: 61.9 us -> none  [the longest x10 19 us: sweep(): jnp.einsum('pij,pjk->pik', ycur, mid, precision=lax.Precision.HIGHEST)]
    pallas_call x0 -> x3, Pallas kernels: none -> 38.5 us  [the longest x1 24.3 us: patch_weights(): pl.pallas_call(weights_kernel, in_specs=[pl.BlockSpec(memory_space=pltpu....]
    gather x4 -> x0, local copies, waits for them, and re-layouts: 25.7 us -> none  [the longest x1 12.3 us: body(): rows = got_rows[slots].reshape(regions_per_processor, -1, breadth_extent)]
    all_to_all x2 -> x0, starting transfers between devices: 19 us -> none  [the longest x1 10.5 us: body(): lax.all_to_all(send_innov.astype(jnp.bfloat16), ('mem', 'patch'), split_a...]
    select_n x5 -> x0, other arithmetic: 14 us -> none  [the longest x1 14 us: body(): jnp.where(valid[:, :, None, None], row_blocks[pick], jnp.zeros((), jnp.bf...]
    convert_element_type x3 -> x0, local copies, waits for them, and re-layouts: 14 us -> none  [the longest x2 10.6 us: body(): prior_average = jnp.mean(state_entries, axis=0, dtype=jnp.float32)]
  transfers between devices with their start and end apart: 3 -> 1, of which waited for: 2 -> 1; matrix products, arithmetic and copies ran while one was open for 14% -> 0% of each run, Pallas kernels for 0% -> 8%
where the time goes in v1:
time: 289 us; the launch traced here: 288 us
  blocking collectives  236 us (82%)
  Pallas kernels  38.5 us (13%)
  local copies, waits for them, and re-layouts  7.7 us (3%)
  starting transfers between devices  3.61 us (1%)
    all_to_all x1, blocking collectives, body(): lax.all_to_all(send, ('mem', 'patch'), split_axis=0, concat_axis=0, tiled...  207 us
    all_to_all x1, blocking collectives, body(): lax.all_to_all(result, 'mem', split_axis=0, concat_axis=1, tiled=True)  28.5 us
    pallas_call x1, Pallas kernels, patch_weights(): pl.pallas_call(weights_kernel, in_specs=[pl.BlockSpec(memory_space=pltpu....  24.3 us
    pallas_call x1, Pallas kernels, send_blocks(): pl.pallas_call(send_kernel, grid=(nb_dev // CHUNK,), in_specs=[pl.BlockSp...  11.7 us
  transfers between devices with their start and end apart: 1, of which 1 were waited for; matrix products, arithmetic and copies ran while one was open for 0% of the time, Pallas kernels for 8%

profile of v1, /device:TPU:2, one launch (start us, length us, event | category | flops | bytes accessed | tf_op | source)
XLA Modules:
  0.0 287.9 jit_solution(8912204768017511833)
XLA Ops:
  0.0 1.0 copy.10
  1.0 0.1 reshape.15.lists_ref
  1.1 0.0 copy-start
  1.1 2.2 copy-done
  3.3 0.0 copy-start.1
  3.3 0.8 copy-done.1
  4.0 0.0 copy-start.2
  4.0 0.8 copy-done.2
  4.8 11.7 %send_blocks.1 = (bf16[128,528,128]{2,1,0:T(8,128)(2,1)}, s32[8,128]{1,0:T(8,128)S(1)}) custom-call(s32[128,128]{1,0:T(8,128)S(1)} %reshape.15.lists_ref, bf16[8192,256]{1,0:T(8,128)(2,1)S(1)} %copy-done, f32[64,128]{1,0:T(8,128)S(1)} %bitcast.15, f32[64,128]{1,0:T(8,128)S(1)} %bitcast.16), custom_call_target="tpu_custom_call" | custom-call | flops 1073741824 | bytes 25165824 | tf_op jit(solution)/shard_map/send_blocks/pallas_call | solution.py:129
  16.5 0.0 copy-start.4
  16.5 207.0 %all_to_all.43.got_ref = bf16[128,528,128]{2,1,0:T(8,128)(2,1)} all-to-all(bf16[128,528,128]{2,1,0:T(8,128)(2,1)} %get-tuple-element.10), channel_id=1, replica_groups=mesh['mem'=4,'patch'=32] {'mem','patch'}, dimensions={0} | all-to-all | bytes 34603008 | tf_op jit(solution)/shard_map/all_to_all | solution.py:330
  223.6 0.0 copy-done.4
  223.6 1.5 copy.16
  225.0 3.6 %all-to-all-start.1 = ((bf16[64,4,4096]{2,0,1:T(8,128)(2,1)}), bf16[64,4,4096]{2,0,1:T(8,128)(2,1)S(1)}, u32[]{:S(2)}, u32[]{:S(2)}) async-start(bf16[64,4,4096]{2,0,1:T(8,128)(2,1)} %bitcast.17), calls=%async_computation.1 | async-start | bytes 4194304 | tf_op jit(solution)/shard_map/all_to_all | solution.py:332
  228.6 0.0 copy-start.3
  228.6 24.3 %patch_weights.1.w_ref = bf16[4,256,256]{2,1,0:T(8,128)(2,1)S(1)} custom-call(s32[8,128]{1,0:T(8,128)S(1)} %get-tuple-element.9.table_ref, bf16[128,528,128]{2,1,0:T(8,128)(2,1)} %all_to_all.43.got_ref), custom_call_target="tpu_custom_call" | custom-call | flops 14227079168 | bytes 67108864 | tf_op jit(solution)/shard_map/patch_weights/pallas_call | solution.py:251
  252.9 2.5 all-to-all-done.1
  255.5 0.0 copy-done.3
  255.5 2.5 analysis.1
  257.9 28.5 %all_to_all.44 = bf16[4,64,4096]{2,1,0:T(8,128)(2,1)S(1)} all-to-all(bf16[4,64,4096]{2,1,0:T(8,128)(2,1)S(1)} %bitcast.14), channel_id=1, replica_groups=mesh['mem'=4,'patch'=32] {'mem'}, dimensions={0} | all-to-all | bytes 4194304 | tf_op jit(solution)/shard_map/all_to_all | solution.py:335
  286.5 1.5 copy.14
Async XLA Ops:
  1.1 2.2 copy-start
  3.3 0.8 copy-start.1
  4.0 0.8 copy-start.2
  16.5 207.0 %copy-start.4 = (bf16[64,16384]{1,0:T(8,128)(2,1)S(1)}, bf16[64,16384]{1,0:T(8,128)(2,1)}, u32[]{:S(2)}) copy-start(bf16[64,16384]{1,0:T(8,128)(2,1)} %param.6) | copy-start | bytes 6291460
  225.0 30.5 %all-to-all-start.1 = ((bf16[64,4,4096]{2,0,1:T(8,128)(2,1)}), bf16[64,4,4096]{2,0,1:T(8,128)(2,1)S(1)}, u32[]{:S(2)}, u32[]{:S(2)}) async-start(bf16[64,4,4096]{2,0,1:T(8,128)(2,1)} %bitcast.17), calls=%async_computation.1 | async-start | bytes 4194304 | tf_op jit(solution)/shard_map/all_to_all | solution.py:332
  228.6 26.9 %copy-start.3 = (s32[512]{0:T(512)S(1)}, s32[512]{0:T(512)}, u32[]{:S(2)}) copy-start(s32[512]{0:T(512)} %tally_ref.1) | copy-start | bytes 6148

commit v2 on v1

v2 whole, which is shorter than its diff:
```python
import math

import jax
import jax.numpy as jnp
from jax import lax
from jax.experimental import pallas as pl
from jax.experimental.pallas import tpu as pltpu
from jax.sharding import PartitionSpec as P

NV = 128
BLK = 128
CAP = 2
ITERS = 10
TAIL = 16
CHUNK = 32
BIG = 1 << 30
LIVE = 4

NT = (((1,), (1,)), ((), ()))
NN = (((1,), (0,)), ((), ()))


def dot(a, b, dims=NN):
    return lax.dot_general(a, b, dims, preferred_element_type=jnp.float32)


def iotas(shape):
    return lax.broadcasted_iota(jnp.int32, shape, 0), lax.broadcasted_iota(jnp.int32, shape, 1)


def send_kernel(
    lists_ref, tally_ref, img_ref, prec_ref, resid_ref, prior_ref, send_ref, table_ref, fields_ref,
    img, prior, wt, innov, tail, square, keys, keys_s,
    img_sems, prior_sem, field_sems, key_sem, tail_sem, sems,
):
    nmem = lax.axis_size("mem")
    npat = lax.axis_size("patch")
    groups = send_ref.shape[0]
    per_patch, patches = lists_ref.shape[0], lists_ref.shape[1] // groups
    members = img.shape[1]
    nb_dev = wt.shape[0]
    steps = nb_dev // CHUNK
    me_m = lax.axis_index("mem")
    me_p = lax.axis_index("patch")
    source = me_m * npat + me_p

    def load(step):
        rows = pl.ds(step * CHUNK * BLK, CHUNK * BLK)
        return pltpu.make_async_copy(img_ref.at[rows, :], img.at[rows, :], img_sems.at[step])

    def place(g):
        return g % nmem * npat + g // nmem

    def field(part):
        extent = fields_ref.shape[2]
        return pltpu.make_async_copy(
            prior.at[:, pl.ds(part * extent, extent)], fields_ref.at[part], field_sems.at[part]
        )

    for step in range(steps):
        load(step).start()
    pltpu.make_async_copy(prior_ref, prior, prior_sem).start()

    blocks = lists_ref[...]
    row, col = iotas(blocks.shape)
    local = blocks - source * nb_dev
    mine = (local >= 0) & (local < nb_dev)
    key = (col % patches * per_patch + row) * nb_dev + local
    first = jnp.min(jnp.where(mine, key, BIG), axis=0, keepdims=True)
    last = jnp.max(jnp.where(mine, key, -1), axis=0, keepdims=True)
    firsts = first = jnp.broadcast_to(first, (8, first.shape[1]))
    lasts = last = jnp.broadcast_to(last, first.shape)
    for q in range(1, patches):
        firsts = jnp.minimum(firsts, pltpu.roll(first, first.shape[1] - q, 1))
        lasts = jnp.maximum(lasts, pltpu.roll(last, last.shape[1] - q, 1))
    keys[0:1, :] = jnp.where(lasts >= 0, firsts % nb_dev, -1)[0:1, :]
    keys[1:2, :] = jnp.where(lasts >= 0, lasts % nb_dev, -1)[0:1, :]
    pltpu.make_async_copy(keys, keys_s, key_sem).start()

    root = jnp.sqrt(prec_ref[...])
    innov[...] = root * resid_ref[...]
    row, col = iotas((members, members))
    centre = (jnp.where(row == col, 1.0, 0.0) - 1.0 / members).astype(jnp.bfloat16)
    pltpu.make_async_copy(keys, keys_s, key_sem).wait()
    row, _ = iotas((TAIL, BLK))

    def fill(g, _):
        one = innov[pl.ds(jnp.maximum(keys_s[0, g * patches], 0), 1), :]
        two = innov[pl.ds(jnp.maximum(keys_s[1, g * patches], 0), 1), :]
        tail[place(g)] = jnp.where(row == 0, one, two).astype(jnp.bfloat16)
        return 0

    lax.fori_loop(0, groups, fill, 0, unroll=8)
    tails = pltpu.make_async_copy(
        tail, send_ref.at[:, pl.ds(CAP * members, TAIL), :], tail_sem
    )
    tails.start()

    for step in range(steps):
        load(step).wait()
        for j in range(step * CHUNK, (step + 1) * CHUNK, 2):
            centred = dot(centre, img[j * BLK : (j + 2) * BLK, :], NT)
            wt[j] = (centred[:, :BLK] * root[j : j + 1, :]).astype(jnp.bfloat16)
            wt[j + 1] = (centred[:, BLK:] * root[j + 1 : j + 2, :]).astype(jnp.bfloat16)

    pltpu.make_async_copy(prior_ref, prior, prior_sem).wait()
    for part in range(fields_ref.shape[0]):
        field(part).start()

    def start(g, _):
        @pl.when(keys_s[0, g * patches] >= 0)
        def _():
            for c in range(CAP):
                pltpu.make_async_copy(
                    wt.at[keys_s[c, g * patches]],
                    send_ref.at[place(g), pl.ds(c * members, members), :],
                    sems.at[g],
                ).start()

        return 0

    lax.fori_loop(0, groups, start, 0, unroll=4)

    my_column = (me_p * nmem + me_m) * patches
    _, col = iotas(blocks.shape)
    _, lane = iotas((per_patch, 128))
    spread = jnp.zeros((per_patch, 128), jnp.int32)
    for q in range(patches):
        held = jnp.where(col == my_column + q, blocks // nb_dev, 0)
        spread = jnp.where(lane == q, jnp.sum(held, axis=1, keepdims=True), spread)
    square[0:per_patch, :] = spread
    turned = square[...].T
    row, col = iotas((per_patch, per_patch))
    for q in range(patches):
        here = turned[q : q + 1, 0:per_patch]
        slot = jnp.zeros_like(here)
        for other in range(q + 1):
            same = spread[:, other : other + 1] == here
            if other == q:
                same = same & (row < col)
            slot = jnp.maximum(slot, jnp.max(jnp.where(same, 1, 0), axis=0, keepdims=True))
        table_ref[q : q + 1, 0:per_patch] = here * CAP + slot
        table_ref[LIVE + q : LIVE + q + 1, :] = jnp.full((1, 128), tally_ref[my_column + q])

    def finish(g, _):
        @pl.when(keys_s[0, g * patches] >= 0)
        def _():
            slots = send_ref.at[place(g), pl.ds(0, CAP * members), :]
            pltpu.make_async_copy(slots, slots, sems.at[g]).wait()

        return 0

    lax.fori_loop(0, groups, finish, 0, unroll=4)
    tails.wait()
    for part in range(fields_ref.shape[0]):
        field(part).wait()


def send_blocks(lists, tally, images, precision, residual, prior, groups, nmem):
    members = images.shape[1]
    nb_dev = images.shape[0] // BLK
    return pl.pallas_call(
        send_kernel,
        in_specs=[
            pl.BlockSpec(memory_space=pltpu.VMEM),
            pl.BlockSpec(memory_space=pltpu.SMEM),
            pl.BlockSpec(memory_space=pl.ANY),
            pl.BlockSpec(memory_space=pltpu.VMEM),
            pl.BlockSpec(memory_space=pltpu.VMEM),
            pl.BlockSpec(memory_space=pl.ANY),
        ],
        out_specs=[
            pl.BlockSpec(memory_space=pl.ANY),
            pl.BlockSpec(memory_space=pltpu.VMEM),
            pl.BlockSpec(memory_space=pl.ANY),
        ],
        out_shape=[
            jax.ShapeDtypeStruct((groups, CAP * members + TAIL, BLK), jnp.bfloat16),
            jax.ShapeDtypeStruct((8, 128), jnp.int32),
            jax.ShapeDtypeStruct(
                (nmem, prior.shape[0], prior.shape[1] // nmem), prior.dtype
            ),
        ],
        scratch_shapes=[
            pltpu.VMEM(images.shape, jnp.bfloat16),
            pltpu.VMEM(prior.shape, jnp.bfloat16),
            pltpu.VMEM((nb_dev, members, BLK), jnp.bfloat16),
            pltpu.VMEM((nb_dev, BLK), jnp.float32),
            pltpu.VMEM((groups, TAIL, BLK), jnp.bfloat16),
            pltpu.VMEM((128, 128), jnp.int32),
            pltpu.VMEM((8, lists.shape[1]), jnp.int32),
            pltpu.SMEM((8, lists.shape[1]), jnp.int32),
            pltpu.SemaphoreType.DMA((nb_dev // CHUNK,)),
            pltpu.SemaphoreType.DMA,
            pltpu.SemaphoreType.DMA((nmem,)),
            pltpu.SemaphoreType.DMA,
            pltpu.SemaphoreType.DMA,
            pltpu.SemaphoreType.DMA((groups,)),
        ],
        compiler_params=pltpu.CompilerParams(vmem_limit_bytes=60 * 2**20),
        cost_estimate=pl.CostEstimate(
            flops=2 * images.shape[0] * members * members,
            bytes_accessed=24 * 2**20,
            transcendentals=0,
        ),
        name="send_blocks",
    )(lists, tally, images, precision, residual, prior)


def split(x):
    high = x.astype(jnp.bfloat16)
    return high, (x - high.astype(jnp.float32)).astype(jnp.bfloat16)


def dot3(a, b):
    ah, al = a
    bh, bl = b
    return dot(
        jnp.concatenate([ah, ah, al], axis=1), jnp.concatenate([bh, bl, bh], axis=0)
    )


def weights_kernel(table_ref, got_ref, out_ref, buf, yh, yl, zh, zl, sems):
    patches = out_ref.shape[0]
    members = out_ref.shape[1]
    per_patch = buf.shape[2] // BLK

    for q in range(patches):

        def fetch(e, _, q=q):
            slot = table_ref[q, e]
            lane = pl.ds(pl.multiple_of(e * BLK, BLK), BLK)
            pltpu.make_async_copy(
                got_ref.at[slot // CAP, pl.ds(pl.multiple_of(slot % CAP * members, members), members), :],
                buf.at[q, pl.ds(0, members), lane],
                sems.at[q],
            ).start()
            pltpu.make_async_copy(
                got_ref.at[slot // CAP, pl.ds(CAP * members, TAIL), :],
                buf.at[q, pl.ds(members, TAIL), lane],
                sems.at[q],
            ).start()
            return 0

        lax.fori_loop(0, per_patch, fetch, 0)

    row, col = iotas((members, members))
    eye = jnp.where(row == col, 1.0, 0.0)
    norms = []
    ybars = []
    for q in range(patches):
        pltpu.make_async_copy(buf.at[q], buf.at[q], sems.at[q]).wait()
        for e in range(per_patch):
            lane = slice(e * BLK, (e + 1) * BLK)
            both = buf[q, members:, lane].astype(jnp.float32)
            second = table_ref[q, e] % CAP == 1
            chosen = jnp.where(second, both[1:2, :], both[0:1, :])
            buf[q, members:, lane] = jnp.broadcast_to(chosen, (TAIL, BLK)).astype(jnp.bfloat16)
        both = dot(buf[q], buf[q, :members, :], NT)
        amat = (members - 1.0) * eye + both[:members]
        norm = jnp.sqrt(jnp.sum(amat * amat, keepdims=True) + 1e-06)
        norms.append(norm)
        ybars.append(both[members : members + 8])
        ysweep = amat / norm
        mid = split(1.5 * eye - 0.5 * ysweep)
        zh[q], zl[q] = mid
        yh[q], yl[q] = split(dot3(split(ysweep), mid))

    def middle(q):
        prod = dot3((zh[q], zl[q]), (yh[q], yl[q]))
        return split(1.5 * eye - 0.5 * prod)

    def sweep(_, carry):
        mids = [middle(q) for q in range(patches)]
        for q in range(patches):
            yh[q], yl[q] = split(dot3((yh[q], yl[q]), mids[q]))
            zh[q], zl[q] = split(dot3(mids[q], (zh[q], zl[q])))
        return carry

    lax.fori_loop(0, ITERS - 2, sweep, 0)
    for q in range(patches):
        root_inv = dot3(middle(q), (zh[q], zl[q])) / jnp.sqrt(norms[q])
        parts = split(root_inv)
        inner = dot3(split(ybars[q]), parts)
        mean_w = dot3(split(inner), parts)[0:1, :]
        out_ref[q] = (math.sqrt(members - 1.0) * root_inv + mean_w).astype(jnp.bfloat16)


def patch_weights(table, got, patches, per_patch, members):
    square = pltpu.VMEM((patches, members, members), jnp.bfloat16)
    return pl.pallas_call(
        weights_kernel,
        in_specs=[
            pl.BlockSpec(memory_space=pltpu.SMEM),
            pl.BlockSpec(memory_space=pl.ANY),
        ],
        out_specs=pl.BlockSpec(memory_space=pltpu.VMEM),
        out_shape=jax.ShapeDtypeStruct((patches, members, members), jnp.bfloat16),
        scratch_shapes=[
            pltpu.VMEM((patches, members + TAIL, per_patch * BLK), jnp.bfloat16),
            square,
            square,
            square,
            square,
            pltpu.SemaphoreType.DMA((patches,)),
        ],
        compiler_params=pltpu.CompilerParams(vmem_limit_bytes=40 * 2**20),
        cost_estimate=pl.CostEstimate(
            flops=2 * patches * members * members * (per_patch * BLK + 90 * members),
            bytes_accessed=64 * 2**20,
            transcendentals=0,
        ),
        name="patch_weights",
    )(table, got)


def analysis_kernel(table_ref, w_ref, x_ref, out_ref):
    live = table_ref[LIVE + pl.program_id(0), 0]
    prior = x_ref[...].astype(jnp.float32)
    mean = jnp.mean(prior, axis=0, keepdims=True)
    anomaly = (prior - mean).astype(jnp.bfloat16)
    blended = mean + dot(w_ref[0], anomaly)
    _, col = iotas((1, x_ref.shape[1]))
    out_ref[...] = jnp.where(col < live * NV, blended, prior).astype(jnp.bfloat16)


def analyse(table, weights, state):
    patches, members, _ = weights.shape
    extent = state.shape[1] // patches
    return pl.pallas_call(
        analysis_kernel,
        grid=(patches,),
        in_specs=[
            pl.BlockSpec(memory_space=pltpu.SMEM),
            pl.BlockSpec((1, members, members), lambda q: (q, 0, 0)),
            pl.BlockSpec((members, extent), lambda q: (0, q)),
        ],
        out_specs=pl.BlockSpec((members, extent), lambda q: (0, q)),
        out_shape=jax.ShapeDtypeStruct(state.shape, jnp.bfloat16),
        compiler_params=pltpu.CompilerParams(vmem_limit_bytes=32 * 2**20),
        cost_estimate=pl.CostEstimate(
            flops=2 * members * members * state.shape[1],
            bytes_accessed=4 * members * state.shape[1],
            transcendentals=0,
        ),
        name="analysis",
    )(table, weights, state)


def body(
    prior_states,
    member_obs_images,
    obs_residual,
    obs_precision_weights,
    region_obs_groups,
    active_profile_tally,
):
    devices = lax.axis_size("mem") * lax.axis_size("patch")
    members = member_obs_images.shape[1]
    patches = region_obs_groups.shape[0] // devices
    nmem = lax.axis_size("mem")
    send, table, fields = send_blocks(
        region_obs_groups.T,
        active_profile_tally,
        member_obs_images,
        obs_precision_weights.reshape(-1, BLK),
        obs_residual.reshape(-1, BLK),
        prior_states,
        devices,
        nmem,
    )
    got = lax.all_to_all(send, ("mem", "patch"), split_axis=0, concat_axis=0, tiled=True)
    got, fields = lax.optimization_barrier((got, fields))
    fields = lax.all_to_all(fields, "mem", split_axis=0, concat_axis=0, tiled=True)
    state = fields.reshape(members, -1)
    weights = patch_weights(table, got, patches, region_obs_groups.shape[1], members)
    result = analyse(table, weights, state)
    return lax.all_to_all(result, "mem", split_axis=0, concat_axis=1, tiled=True)


def solution(mesh):
    return jax.shard_map(
        body,
        mesh=mesh,
        in_specs=(
            P("mem", "patch"),
            P(("mem", "patch"), None),
            P(("mem", "patch")),
            P(("mem", "patch")),
            P(),
            P(),
        ),
        out_specs=P("mem", "patch"),
        check_vma=False,
    )
```

time: 289 us -> 281 us (0.972)
  local copies, waits for them, and re-layouts: 7.7 us -> 1.46 us
    unnamed x11 -> x2, local copies, waits for them, and re-layouts: 4.67 us -> 0.01 us
  transfers between devices with their start and end apart: 1 -> 1, of which waited for: 1 -> 1; matrix products, arithmetic and copies ran while one was open for 0% -> 0% of each run, Pallas kernels for 8% -> 9%
where the time goes in v2:
time: 281 us
  blocking collectives  236 us (84%)
  Pallas kernels  37.3 us (13%)
  starting transfers between devices  3.74 us (1%)
    all_to_all x1, blocking collectives, body(): lax.all_to_all(send, ('mem', 'patch'), split_axis=0, concat_axis=0, tiled...  207 us
    all_to_all x1, blocking collectives, body(): lax.all_to_all(result, 'mem', split_axis=0, concat_axis=1, tiled=True)  28.5 us
    pallas_call x1, Pallas kernels, patch_weights(): pl.pallas_call(weights_kernel, in_specs=[pl.BlockSpec(memory_space=pltpu....  24.4 us
    pallas_call x1, Pallas kernels, send_blocks(): pl.pallas_call(send_kernel, in_specs=[pl.BlockSpec(memory_space=pltpu.VME...  10.4 us
  transfers between devices with their start and end apart: 1, of which 1 were waited for; matrix products, arithmetic and copies ran while one was open for 0% of the time, Pallas kernels for 9%

profile of v2, /device:TPU:2, one launch (start us, length us, event | category | flops | bytes accessed | tf_op | source)
XLA Modules:
  0.0 280.6 jit_solution(9712899234480152599)
XLA Ops:
  0.0 10.4 %send_blocks.1 = (bf16[128,528,128]{2,1,0:T(8,128)(2,1)}, s32[8,128]{1,0:T(8,128)}, bf16[4,64,4096]{2,1,0:T(8,128)(2,1)}) custom-call(s32[32,512]{1,0:T(8,128)} %bitcast.11, s32[512]{0:T(512)} %tally_ref.1, bf16[8192,256]{1,0:T(8,128)(2,1)} %img_ref.1, f32[64,128]{1,0:T(8,128)} %bitcast.12, f32[64,128]{1,0:T(8,128)} %bitcast.13, bf16[64,16384]{1,0:T(8,128)(2,1)} %prior_ref.1), custom_call_target="tpu_custom_call" | custom-call | flops 1073741824 | bytes 25165824 | tf_op jit(solution)/shard_map/send_blocks/pallas_call | solution.py:162
  10.4 207.1 %all_to_all.29.got_ref = bf16[128,528,128]{2,1,0:T(8,128)(2,1)} all-to-all(bf16[128,528,128]{2,1,0:T(8,128)(2,1)} %get-tuple-element.11), channel_id=1, replica_groups=mesh['mem'=4,'patch'=32] {'mem','patch'}, dimensions={0} | all-to-all | bytes 34603008 | tf_op jit(solution)/shard_map/all_to_all | solution.py:372
  217.5 0.0 copy-start
  217.5 3.7 %all-to-all-start.1 = ((bf16[4,64,4096]{2,1,0:T(8,128)(2,1)}), bf16[4,64,4096]{2,1,0:T(8,128)(2,1)S(1)}, u32[]{:S(2)}, u32[]{:S(2)}) async-start(bf16[4,64,4096]{2,1,0:T(8,128)(2,1)} %get-tuple-element.14), calls=%async_computation.1 | async-start | bytes 4194304 | tf_op jit(solution)/shard_map/all_to_all | solution.py:374
  221.2 0.0 copy-done
  221.3 24.4 %patch_weights.1.w_ref = bf16[4,256,256]{2,1,0:T(8,128)(2,1)S(1)} custom-call(s32[8,128]{1,0:T(8,128)S(1)} %copy-done, bf16[128,528,128]{2,1,0:T(8,128)(2,1)} %all_to_all.29.got_ref), custom_call_target="tpu_custom_call" | custom-call | flops 14227079168 | bytes 67108864 | tf_op jit(solution)/shard_map/patch_weights/pallas_call | solution.py:291
  245.7 2.4 all-to-all-done.1
  248.1 2.5 analysis.1
  250.6 28.5 %all_to_all.30 = bf16[4,64,4096]{2,1,0:T(8,128)(2,1)S(1)} all-to-all(bf16[4,64,4096]{2,1,0:T(8,128)(2,1)S(1)} %bitcast.9), channel_id=1, replica_groups=mesh['mem'=4,'patch'=32] {'mem'}, dimensions={0} | all-to-all | bytes 4194304 | tf_op jit(solution)/shard_map/all_to_all | solution.py:378
  279.1 1.5 copy.8
Async XLA Ops:
  217.5 3.8 %copy-start = (s32[8,128]{1,0:T(8,128)S(1)}, s32[8,128]{1,0:T(8,128)}, u32[]{:S(2)}) copy-start(s32[8,128]{1,0:T(8,128)} %get-tuple-element.10.table_ref) | copy-start | bytes 12292
  217.5 30.6 %all-to-all-start.1 = ((bf16[4,64,4096]{2,1,0:T(8,128)(2,1)}), bf16[4,64,4096]{2,1,0:T(8,128)(2,1)S(1)}, u32[]{:S(2)}, u32[]{:S(2)}) async-start(bf16[4,64,4096]{2,1,0:T(8,128)(2,1)} %get-tuple-element.14), calls=%async_computation.1 | async-start | bytes 4194304 | tf_op jit(solution)/shard_map/all_to_all | solution.py:374

commit v3 on v2

--- a/solution.py
+++ b/solution.py
@@ -15,6 +15,7 @@
 CHUNK = 32
 BIG = 1 << 30
 LIVE = 4
+RUN = 32
 
 NT = (((1,), (1,)), ((), ()))
 NN = (((1,), (0,)), ((), ()))
@@ -48,8 +49,13 @@
         rows = pl.ds(step * CHUNK * BLK, CHUNK * BLK)
         return pltpu.make_async_copy(img_ref.at[rows, :], img.at[rows, :], img_sems.at[step])
 
-    def place(g):
-        return g % nmem * npat + g // nmem
+    def each(act):
+        def column(p, _):
+            for m in range(nmem):
+                act(p * nmem + m, m * npat + p)
+            return 0
+
+        lax.fori_loop(0, npat, column, 0, unroll=2)
 
     def field(part):
         extent = fields_ref.shape[2]
@@ -84,13 +90,12 @@
     pltpu.make_async_copy(keys, keys_s, key_sem).wait()
     row, _ = iotas((TAIL, BLK))
 
-    def fill(g, _):
+    def fill(g, dest):
         one = innov[pl.ds(jnp.maximum(keys_s[0, g * patches], 0), 1), :]
         two = innov[pl.ds(jnp.maximum(keys_s[1, g * patches], 0), 1), :]
-        tail[place(g)] = jnp.where(row == 0, one, two).astype(jnp.bfloat16)
-        return 0
-
-    lax.fori_loop(0, groups, fill, 0, unroll=8)
+        tail[dest] = jnp.where(row == 0, one, two).astype(jnp.bfloat16)
+
+    each(fill)
     tails = pltpu.make_async_copy(
         tail, send_ref.at[:, pl.ds(CAP * members, TAIL), :], tail_sem
     )
@@ -107,19 +112,17 @@
     for part in range(fields_ref.shape[0]):
         field(part).start()
 
-    def start(g, _):
+    def start(g, dest):
         @pl.when(keys_s[0, g * patches] >= 0)
         def _():
             for c in range(CAP):
                 pltpu.make_async_copy(
                     wt.at[keys_s[c, g * patches]],
-                    send_ref.at[place(g), pl.ds(c * members, members), :],
+                    send_ref.at[dest, pl.ds(c * members, members), :],
                     sems.at[g],
                 ).start()
 
-        return 0
-
-    lax.fori_loop(0, groups, start, 0, unroll=4)
+    each(start)
 
     my_column = (me_p * nmem + me_m) * patches
     _, col = iotas(blocks.shape)
@@ -142,15 +145,13 @@
         table_ref[q : q + 1, 0:per_patch] = here * CAP + slot
         table_ref[LIVE + q : LIVE + q + 1, :] = jnp.full((1, 128), tally_ref[my_column + q])
 
-    def finish(g, _):
+    def finish(g, dest):
         @pl.when(keys_s[0, g * patches] >= 0)
         def _():
-            slots = send_ref.at[place(g), pl.ds(0, CAP * members), :]
+            slots = send_ref.at[dest, pl.ds(0, CAP * members), :]
             pltpu.make_async_copy(slots, slots, sems.at[g]).wait()
 
-        return 0
-
-    lax.fori_loop(0, groups, finish, 0, unroll=4)
+    each(finish)
     tails.wait()
     for part in range(fields_ref.shape[0]):
         field(part).wait()
@@ -220,43 +221,48 @@
     )
 
 
-def weights_kernel(table_ref, got_ref, out_ref, buf, yh, yl, zh, zl, sems):
+def weights_kernel(table_ref, got_ref, out_ref, buf, tails, yh, yl, zh, zl, tail_sem, sems):
     patches = out_ref.shape[0]
     members = out_ref.shape[1]
-    per_patch = buf.shape[2] // BLK
-
+    per_patch = buf.shape[1]
+
+    tailing = pltpu.make_async_copy(
+        got_ref.at[:, pl.ds(CAP * members, TAIL), :], tails, tail_sem
+    )
+    tailing.start()
     for q in range(patches):
 
         def fetch(e, _, q=q):
             slot = table_ref[q, e]
-            lane = pl.ds(pl.multiple_of(e * BLK, BLK), BLK)
+            first = pl.multiple_of(jnp.bitwise_and(slot, CAP - 1) * members, members)
             pltpu.make_async_copy(
-                got_ref.at[slot // CAP, pl.ds(pl.multiple_of(slot % CAP * members, members), members), :],
-                buf.at[q, pl.ds(0, members), lane],
-                sems.at[q],
-            ).start()
-            pltpu.make_async_copy(
-                got_ref.at[slot // CAP, pl.ds(CAP * members, TAIL), :],
-                buf.at[q, pl.ds(members, TAIL), lane],
+                got_ref.at[lax.shift_right_logical(slot, 1), pl.ds(first, members), :],
+                buf.at[q, e],
                 sems.at[q],
             ).start()
             return 0
 
-        lax.fori_loop(0, per_patch, fetch, 0)
+        lax.fori_loop(0, per_patch, fetch, 0, unroll=8)
+    tailing.wait()
 
     row, col = iotas((members, members))
     eye = jnp.where(row == col, 1.0, 0.0)
     norms = []
     ybars = []
     for q in range(patches):
+        both = jnp.zeros((members + TAIL, members), jnp.float32)
+        scaled = []
+        for e in range(per_patch):
+            slot = table_ref[q, e]
+            pair = tails[lax.shift_right_logical(slot, 1)].astype(jnp.float32)
+            chosen = jnp.where(jnp.bitwise_and(slot, 1) == 1, pair[1:2, :], pair[0:1, :])
+            scaled.append(jnp.broadcast_to(chosen, (TAIL, BLK)).astype(jnp.bfloat16))
         pltpu.make_async_copy(buf.at[q], buf.at[q], sems.at[q]).wait()
-        for e in range(per_patch):
-            lane = slice(e * BLK, (e + 1) * BLK)
-            both = buf[q, members:, lane].astype(jnp.float32)
-            second = table_ref[q, e] % CAP == 1
-            chosen = jnp.where(second, both[1:2, :], both[0:1, :])
-            buf[q, members:, lane] = jnp.broadcast_to(chosen, (TAIL, BLK)).astype(jnp.bfloat16)
-        both = dot(buf[q], buf[q, :members, :], NT)
+        for lo in range(0, per_patch, RUN):
+            run = range(lo, min(lo + RUN, per_patch))
+            rows = jnp.concatenate([buf[q, e] for e in run], axis=1)
+            extra = jnp.concatenate([scaled[e] for e in run], axis=1)
+            both = both + dot(jnp.concatenate([rows, extra], axis=0), rows, NT)
         amat = (members - 1.0) * eye + both[:members]
         norm = jnp.sqrt(jnp.sum(amat * amat, keepdims=True) + 1e-06)
         norms.append(norm)
@@ -277,7 +283,7 @@
             zh[q], zl[q] = split(dot3(mids[q], (zh[q], zl[q])))
         return carry
 
-    lax.fori_loop(0, ITERS - 2, sweep, 0)
+    lax.fori_loop(0, ITERS - 2, sweep, 0, unroll=2)
     for q in range(patches):
         root_inv = dot3(middle(q), (zh[q], zl[q])) / jnp.sqrt(norms[q])
         parts = split(root_inv)
@@ -297,11 +303,13 @@
         out_specs=pl.BlockSpec(memory_space=pltpu.VMEM),
         out_shape=jax.ShapeDtypeStruct((patches, members, members), jnp.bfloat16),
         scratch_shapes=[
-            pltpu.VMEM((patches, members + TAIL, per_patch * BLK), jnp.bfloat16),
+            pltpu.VMEM((patches, per_patch, members, BLK), jnp.bfloat16),
+            pltpu.VMEM((got.shape[0], TAIL, BLK), jnp.bfloat16),
             square,
             square,
             square,
             square,
+            pltpu.SemaphoreType.DMA,
             pltpu.SemaphoreType.DMA((patches,)),
         ],
         compiler_params=pltpu.CompilerParams(vmem_limit_bytes=40 * 2**20),
@@ -315,27 +323,29 @@
 
 
 def analysis_kernel(table_ref, w_ref, x_ref, out_ref):
-    live = table_ref[LIVE + pl.program_id(0), 0]
-    prior = x_ref[...].astype(jnp.float32)
-    mean = jnp.mean(prior, axis=0, keepdims=True)
-    anomaly = (prior - mean).astype(jnp.bfloat16)
-    blended = mean + dot(w_ref[0], anomaly)
-    _, col = iotas((1, x_ref.shape[1]))
-    out_ref[...] = jnp.where(col < live * NV, blended, prior).astype(jnp.bfloat16)
+    patches = w_ref.shape[0]
+    extent = x_ref.shape[1] // patches
+    _, col = iotas((1, extent))
+    for q in range(patches):
+        span = slice(q * extent, (q + 1) * extent)
+        prior = x_ref[:, span].astype(jnp.float32)
+        mean = jnp.mean(prior, axis=0, keepdims=True)
+        anomaly = (prior - mean).astype(jnp.bfloat16)
+        blended = mean + dot(w_ref[q], anomaly)
+        live = col < table_ref[LIVE + q, 0] * NV
+        out_ref[:, span] = jnp.where(live, blended, prior).astype(jnp.bfloat16)
 
 
 def analyse(table, weights, state):
     patches, members, _ = weights.shape
-    extent = state.shape[1] // patches
     return pl.pallas_call(
         analysis_kernel,
-        grid=(patches,),
         in_specs=[
             pl.BlockSpec(memory_space=pltpu.SMEM),
-            pl.BlockSpec((1, members, members), lambda q: (q, 0, 0)),
-            pl.BlockSpec((members, extent), lambda q: (0, q)),
-        ],
-        out_specs=pl.BlockSpec((members, extent), lambda q: (0, q)),
+            pl.BlockSpec(memory_space=pltpu.VMEM),
+            pl.BlockSpec(memory_space=pltpu.VMEM),
+        ],
+        out_specs=pl.BlockSpec(memory_space=pltpu.VMEM),
         out_shape=jax.ShapeDtypeStruct(state.shape, jnp.bfloat16),
         compiler_params=pltpu.CompilerParams(vmem_limit_bytes=32 * 2**20),
         cost_estimate=pl.CostEstimate(

time: 281 us -> 280 us (level)
  transfers between devices with their start and end apart: 1 -> 1, of which waited for: 1 -> 1; matrix products, arithmetic and copies ran while one was open for 0% -> 0% of each run, Pallas kernels for 9% -> 8%
where the time goes in v3:
time: 280 us
  blocking collectives  236 us (84%)
  Pallas kernels  35.3 us (13%)
  starting transfers between devices  3.74 us (1%)
  waiting for transfers between devices  3.49 us (1%)
    all_to_all x1, blocking collectives, body(): lax.all_to_all(send, ('mem', 'patch'), split_axis=0, concat_axis=0, tiled...  207 us
    all_to_all x1, blocking collectives, body(): lax.all_to_all(result, 'mem', split_axis=0, concat_axis=1, tiled=True)  28.5 us
    pallas_call x1, Pallas kernels, patch_weights(): pl.pallas_call(weights_kernel, in_specs=[pl.BlockSpec(memory_space=pltpu....  23.4 us
    pallas_call x1, Pallas kernels, send_blocks(): pl.pallas_call(send_kernel, in_specs=[pl.BlockSpec(memory_space=pltpu.VME...  9.88 us
  transfers between devices with their start and end apart: 1, of which 1 were waited for; matrix products, arithmetic and copies ran while one was open for 0% of the time, Pallas kernels for 8%

profile of v3, /device:TPU:2, one launch (start us, length us, event | category | flops | bytes accessed | tf_op | source)
XLA Modules:
  0.0 279.5 jit_solution(17861710551452506803)
XLA Ops:
  0.0 9.9 %send_blocks.1 = (bf16[128,528,128]{2,1,0:T(8,128)(2,1)}, s32[8,128]{1,0:T(8,128)}, bf16[4,64,4096]{2,1,0:T(8,128)(2,1)}) custom-call(s32[32,512]{1,0:T(8,128)} %bitcast.11, s32[512]{0:T(512)} %tally_ref.1, bf16[8192,256]{1,0:T(8,128)(2,1)} %img_ref.1, f32[64,128]{1,0:T(8,128)} %bitcast.12, f32[64,128]{1,0:T(8,128)} %bitcast.13, bf16[64,16384]{1,0:T(8,128)(2,1)} %prior_ref.1), custom_call_target="tpu_custom_call" | custom-call | flops 1073741824 | bytes 25165824 | tf_op jit(solution)/shard_map/send_blocks/pallas_call | solution.py:163
  9.9 207.0 %all_to_all.29.got_ref = bf16[128,528,128]{2,1,0:T(8,128)(2,1)} all-to-all(bf16[128,528,128]{2,1,0:T(8,128)(2,1)} %get-tuple-element.11), channel_id=1, replica_groups=mesh['mem'=4,'patch'=32] {'mem','patch'}, dimensions={0} | all-to-all | bytes 34603008 | tf_op jit(solution)/shard_map/all_to_all | solution.py:382
  216.9 0.0 copy-start
  216.9 3.7 %all-to-all-start.1 = ((bf16[4,64,4096]{2,1,0:T(8,128)(2,1)}), bf16[4,64,4096]{2,1,0:T(8,128)(2,1)S(1)}, u32[]{:S(2)}, u32[]{:S(2)}) async-start(bf16[4,64,4096]{2,1,0:T(8,128)(2,1)} %get-tuple-element.14), calls=%async_computation.1 | async-start | bytes 4194304 | tf_op jit(solution)/shard_map/all_to_all | solution.py:384
  220.6 0.0 copy-done
  220.6 23.4 %patch_weights.1.w_ref = bf16[4,256,256]{2,1,0:T(8,128)(2,1)S(1)} custom-call(s32[8,128]{1,0:T(8,128)S(1)} %copy-done, bf16[128,528,128]{2,1,0:T(8,128)(2,1)} %all_to_all.29.got_ref), custom_call_target="tpu_custom_call" | custom-call | flops 14227079168 | bytes 67108864 | tf_op jit(solution)/shard_map/patch_weights/pallas_call | solution.py:297
  244.0 3.5 %all-to-all-done.1 = bf16[4,64,4096]{2,1,0:T(8,128)(2,1)S(1)} async-done(((bf16[4,64,4096]{2,1,0:T(8,128)(2,1)}), bf16[4,64,4096]{2,1,0:T(8,128)(2,1)S(1)}, u32[]{:S(2)}, u32[]{:S(2)}) %all-to-all-start.1) | async-done | bytes 2097184 | tf_op jit(solution)/shard_map/all_to_all | solution.py:384
  247.5 2.1 analysis.1
  249.6 28.5 %all_to_all.30 = bf16[4,64,4096]{2,1,0:T(8,128)(2,1)S(1)} all-to-all(bf16[4,64,4096]{2,1,0:T(8,128)(2,1)S(1)} %bitcast.9), channel_id=1, replica_groups=mesh['mem'=4,'patch'=32] {'mem'}, dimensions={0} | all-to-all | bytes 4194304 | tf_op jit(solution)/shard_map/all_to_all | solution.py:388
  278.1 1.5 copy.8
Async XLA Ops:
  216.9 3.8 %copy-start = (s32[8,128]{1,0:T(8,128)S(1)}, s32[8,128]{1,0:T(8,128)}, u32[]{:S(2)}) copy-start(s32[8,128]{1,0:T(8,128)} %get-tuple-element.10.table_ref) | copy-start | bytes 12292
  216.9 30.6 %all-to-all-start.1 = ((bf16[4,64,4096]{2,1,0:T(8,128)(2,1)}), bf16[4,64,4096]{2,1,0:T(8,128)(2,1)S(1)}, u32[]{:S(2)}, u32[]{:S(2)}) async-start(bf16[4,64,4096]{2,1,0:T(8,128)(2,1)} %get-tuple-element.14), calls=%async_computation.1 | async-start | bytes 4194304 | tf_op jit(solution)/shard_map/all_to_all | solution.py:384

commit v4 on v3

--- a/solution.py
+++ b/solution.py
@@ -11,11 +11,13 @@
 BLK = 128
 CAP = 2
 ITERS = 10
-TAIL = 16
+TAIL = 8
 CHUNK = 32
 BIG = 1 << 30
 LIVE = 4
 RUN = 32
+AHEAD = 4
+EXTRA = 16
 
 NT = (((1,), (1,)), ((), ()))
 NN = (((1,), (0,)), ((), ()))
@@ -230,9 +232,9 @@
         got_ref.at[:, pl.ds(CAP * members, TAIL), :], tails, tail_sem
     )
     tailing.start()
-    for q in range(patches):
-
-        def fetch(e, _, q=q):
+
+    def gather(q):
+        def fetch(e, _):
             slot = table_ref[q, e]
             first = pl.multiple_of(jnp.bitwise_and(slot, CAP - 1) * members, members)
             pltpu.make_async_copy(
@@ -243,6 +245,9 @@
             return 0
 
         lax.fori_loop(0, per_patch, fetch, 0, unroll=8)
+
+    for q in range(min(AHEAD, patches)):
+        gather(q)
     tailing.wait()
 
     row, col = iotas((members, members))
@@ -250,14 +255,16 @@
     norms = []
     ybars = []
     for q in range(patches):
-        both = jnp.zeros((members + TAIL, members), jnp.float32)
+        both = jnp.zeros((members + EXTRA, members), jnp.float32)
         scaled = []
         for e in range(per_patch):
             slot = table_ref[q, e]
             pair = tails[lax.shift_right_logical(slot, 1)].astype(jnp.float32)
             chosen = jnp.where(jnp.bitwise_and(slot, 1) == 1, pair[1:2, :], pair[0:1, :])
-            scaled.append(jnp.broadcast_to(chosen, (TAIL, BLK)).astype(jnp.bfloat16))
+            scaled.append(jnp.broadcast_to(chosen, (EXTRA, BLK)).astype(jnp.bfloat16))
         pltpu.make_async_copy(buf.at[q], buf.at[q], sems.at[q]).wait()
+        if q + AHEAD < patches:
+            gather(q + AHEAD)
         for lo in range(0, per_patch, RUN):
             run = range(lo, min(lo + RUN, per_patch))
             rows = jnp.concatenate([buf[q, e] for e in run], axis=1)

time: 280 us -> 277 us (0.989)
  blocking collectives: 236 us -> 233 us
where the time goes in v4:
time: 277 us
  blocking collectives  233 us (84%)
  Pallas kernels  35 us (13%)
  starting transfers between devices  3.74 us (1%)
  waiting for transfers between devices  3.5 us (1%)
    all_to_all x1, blocking collectives, body(): lax.all_to_all(send, ('mem', 'patch'), split_axis=0, concat_axis=0, tiled...  205 us
    all_to_all x1, blocking collectives, body(): lax.all_to_all(result, 'mem', split_axis=0, concat_axis=1, tiled=True)  28.5 us
    pallas_call x1, Pallas kernels, patch_weights(): pl.pallas_call(weights_kernel, in_specs=[pl.BlockSpec(memory_space=pltpu....  23.3 us
    pallas_call x1, Pallas kernels, send_blocks(): pl.pallas_call(send_kernel, in_specs=[pl.BlockSpec(memory_space=pltpu.VME...  9.61 us
  transfers between devices with their start and end apart: 1, of which 1 were waited for; matrix products, arithmetic and copies ran while one was open for 0% of the time, Pallas kernels for 8%

profile of v4, /device:TPU:2, one launch (start us, length us, event | category | flops | bytes accessed | tf_op | source)
XLA Modules:
  0.0 276.9 jit_solution(11216878442092393457)
XLA Ops:
  0.0 9.6 %send_blocks.1 = (bf16[128,520,128]{2,1,0:T(8,128)(2,1)}, s32[8,128]{1,0:T(8,128)}, bf16[4,64,4096]{2,1,0:T(8,128)(2,1)}) custom-call(s32[32,512]{1,0:T(8,128)} %bitcast.11, s32[512]{0:T(512)} %tally_ref.1, bf16[8192,256]{1,0:T(8,128)(2,1)} %img_ref.1, f32[64,128]{1,0:T(8,128)} %bitcast.12, f32[64,128]{1,0:T(8,128)} %bitcast.13, bf16[64,16384]{1,0:T(8,128)(2,1)} %prior_ref.1), custom_call_target="tpu_custom_call" | custom-call | flops 1073741824 | bytes 25165824 | tf_op jit(solution)/shard_map/send_blocks/pallas_call | solution.py:165
  9.6 204.6 %all_to_all.29.got_ref = bf16[128,520,128]{2,1,0:T(8,128)(2,1)} all-to-all(bf16[128,520,128]{2,1,0:T(8,128)(2,1)} %get-tuple-element.11), channel_id=1, replica_groups=mesh['mem'=4,'patch'=32] {'mem','patch'}, dimensions={0} | all-to-all | bytes 34078720 | tf_op jit(solution)/shard_map/all_to_all | solution.py:389
  214.2 0.0 copy-start
  214.2 3.7 %all-to-all-start.1 = ((bf16[4,64,4096]{2,1,0:T(8,128)(2,1)}), bf16[4,64,4096]{2,1,0:T(8,128)(2,1)S(1)}, u32[]{:S(2)}, u32[]{:S(2)}) async-start(bf16[4,64,4096]{2,1,0:T(8,128)(2,1)} %get-tuple-element.14), calls=%async_computation.1 | async-start | bytes 4194304 | tf_op jit(solution)/shard_map/all_to_all | solution.py:391
  218.0 0.0 copy-done
  218.0 23.3 %patch_weights.1.w_ref = bf16[4,256,256]{2,1,0:T(8,128)(2,1)S(1)} custom-call(s32[8,128]{1,0:T(8,128)S(1)} %copy-done, bf16[128,520,128]{2,1,0:T(8,128)(2,1)} %all_to_all.29.got_ref), custom_call_target="tpu_custom_call" | custom-call | flops 14227079168 | bytes 67108864 | tf_op jit(solution)/shard_map/patch_weights/pallas_call | solution.py:304
  241.3 3.5 %all-to-all-done.1 = bf16[4,64,4096]{2,1,0:T(8,128)(2,1)S(1)} async-done(((bf16[4,64,4096]{2,1,0:T(8,128)(2,1)}), bf16[4,64,4096]{2,1,0:T(8,128)(2,1)S(1)}, u32[]{:S(2)}, u32[]{:S(2)}) %all-to-all-start.1) | async-done | bytes 2097184 | tf_op jit(solution)/shard_map/all_to_all | solution.py:391
  244.8 2.1 analysis.1
  246.9 28.5 %all_to_all.30 = bf16[4,64,4096]{2,1,0:T(8,128)(2,1)S(1)} all-to-all(bf16[4,64,4096]{2,1,0:T(8,128)(2,1)S(1)} %bitcast.9), channel_id=1, replica_groups=mesh['mem'=4,'patch'=32] {'mem'}, dimensions={0} | all-to-all | bytes 4194304 | tf_op jit(solution)/shard_map/all_to_all | solution.py:395
  275.4 1.5 copy.8
Async XLA Ops:
  214.2 3.8 %copy-start = (s32[8,128]{1,0:T(8,128)S(1)}, s32[8,128]{1,0:T(8,128)}, u32[]{:S(2)}) copy-start(s32[8,128]{1,0:T(8,128)} %get-tuple-element.10.table_ref) | copy-start | bytes 12292
  214.2 30.6 %all-to-all-start.1 = ((bf16[4,64,4096]{2,1,0:T(8,128)(2,1)}), bf16[4,64,4096]{2,1,0:T(8,128)(2,1)S(1)}, u32[]{:S(2)}, u32[]{:S(2)}) async-start(bf16[4,64,4096]{2,1,0:T(8,128)(2,1)} %get-tuple-element.14), calls=%async_computation.1 | async-start | bytes 4194304 | tf_op jit(solution)/shard_map/all_to_all | solution.py:391

commit v5 on v4

--- a/solution.py
+++ b/solution.py
@@ -332,15 +332,17 @@
 def analysis_kernel(table_ref, w_ref, x_ref, out_ref):
     patches = w_ref.shape[0]
     extent = x_ref.shape[1] // patches
+    members = x_ref.shape[0]
     _, col = iotas((1, extent))
+    average = jnp.full((EXTRA, members), 1.0 / members, jnp.bfloat16)
     for q in range(patches):
         span = slice(q * extent, (q + 1) * extent)
-        prior = x_ref[:, span].astype(jnp.float32)
-        mean = jnp.mean(prior, axis=0, keepdims=True)
-        anomaly = (prior - mean).astype(jnp.bfloat16)
-        blended = mean + dot(w_ref[q], anomaly)
+        prior = x_ref[:, span]
+        both = dot(jnp.concatenate([w_ref[q], average], axis=0), prior)
+        rest = 1.0 - jnp.sum(w_ref[q].astype(jnp.float32), axis=1, keepdims=True)
+        blended = (both[:members] + rest * both[members : members + 1]).astype(jnp.bfloat16)
         live = col < table_ref[LIVE + q, 0] * NV
-        out_ref[:, span] = jnp.where(live, blended, prior).astype(jnp.bfloat16)
+        out_ref[:, span] = jnp.where(live, blended, prior)
 
 
 def analyse(table, weights, state):

time: 277 us -> 277 us (level)
  no operation moved by 1% of the time
where the time goes in v5:
time: 277 us; the launch traced here: 276 us
  blocking collectives  233 us (84%)
  Pallas kernels  34.8 us (13%)
  starting transfers between devices  3.74 us (1%)
  waiting for transfers between devices  3.51 us (1%)
    all_to_all x1, blocking collectives, body(): lax.all_to_all(send, ('mem', 'patch'), split_axis=0, concat_axis=0, tiled...  204 us
    all_to_all x1, blocking collectives, body(): lax.all_to_all(result, 'mem', split_axis=0, concat_axis=1, tiled=True)  28.5 us
    pallas_call x1, Pallas kernels, patch_weights(): pl.pallas_call(weights_kernel, in_specs=[pl.BlockSpec(memory_space=pltpu....  23.3 us
    pallas_call x1, Pallas kernels, send_blocks(): pl.pallas_call(send_kernel, in_specs=[pl.BlockSpec(memory_space=pltpu.VME...  9.5 us
  transfers between devices with their start and end apart: 1, of which 1 were waited for; matrix products, arithmetic and copies ran while one was open for 0% of the time, Pallas kernels for 8%

profile of v5, /device:TPU:2, one launch (start us, length us, event | category | flops | bytes accessed | tf_op | source)
XLA Modules:
  0.0 276.4 jit_solution(3999764361007150879)
XLA Ops:
  0.0 9.5 %send_blocks.1 = (bf16[128,520,128]{2,1,0:T(8,128)(2,1)}, s32[8,128]{1,0:T(8,128)}, bf16[4,64,4096]{2,1,0:T(8,128)(2,1)}) custom-call(s32[32,512]{1,0:T(8,128)} %bitcast.11, s32[512]{0:T(512)} %tally_ref.1, bf16[8192,256]{1,0:T(8,128)(2,1)} %img_ref.1, f32[64,128]{1,0:T(8,128)} %bitcast.12, f32[64,128]{1,0:T(8,128)} %bitcast.13, bf16[64,16384]{1,0:T(8,128)(2,1)} %prior_ref.1), custom_call_target="tpu_custom_call" | custom-call | flops 1073741824 | bytes 25165824 | tf_op jit(solution)/shard_map/send_blocks/pallas_call | solution.py:165
  9.5 204.4 %all_to_all.29.got_ref = bf16[128,520,128]{2,1,0:T(8,128)(2,1)} all-to-all(bf16[128,520,128]{2,1,0:T(8,128)(2,1)} %get-tuple-element.11), channel_id=1, replica_groups=mesh['mem'=4,'patch'=32] {'mem','patch'}, dimensions={0} | all-to-all | bytes 34078720 | tf_op jit(solution)/shard_map/all_to_all | solution.py:391
  213.9 0.0 copy-start
  213.9 3.7 %all-to-all-start.1 = ((bf16[4,64,4096]{2,1,0:T(8,128)(2,1)}), bf16[4,64,4096]{2,1,0:T(8,128)(2,1)S(1)}, u32[]{:S(2)}, u32[]{:S(2)}) async-start(bf16[4,64,4096]{2,1,0:T(8,128)(2,1)} %get-tuple-element.14), calls=%async_computation.1 | async-start | bytes 4194304 | tf_op jit(solution)/shard_map/all_to_all | solution.py:393
  217.6 0.0 copy-done
  217.6 23.3 %patch_weights.1.w_ref = bf16[4,256,256]{2,1,0:T(8,128)(2,1)S(1)} custom-call(s32[8,128]{1,0:T(8,128)S(1)} %copy-done, bf16[128,520,128]{2,1,0:T(8,128)(2,1)} %all_to_all.29.got_ref), custom_call_target="tpu_custom_call" | custom-call | flops 14227079168 | bytes 67108864 | tf_op jit(solution)/shard_map/patch_weights/pallas_call | solution.py:304
  241.0 3.5 %all-to-all-done.1 = bf16[4,64,4096]{2,1,0:T(8,128)(2,1)S(1)} async-done(((bf16[4,64,4096]{2,1,0:T(8,128)(2,1)}), bf16[4,64,4096]{2,1,0:T(8,128)(2,1)S(1)}, u32[]{:S(2)}, u32[]{:S(2)}) %all-to-all-start.1) | async-done | bytes 2097184 | tf_op jit(solution)/shard_map/all_to_all | solution.py:393
  244.5 1.9 analysis.1
  246.4 28.5 %all_to_all.30 = bf16[4,64,4096]{2,1,0:T(8,128)(2,1)S(1)} all-to-all(bf16[4,64,4096]{2,1,0:T(8,128)(2,1)S(1)} %bitcast.9), channel_id=1, replica_groups=mesh['mem'=4,'patch'=32] {'mem'}, dimensions={0} | all-to-all | bytes 4194304 | tf_op jit(solution)/shard_map/all_to_all | solution.py:397
  274.9 1.5 copy.8
Async XLA Ops:
  213.9 3.8 %copy-start = (s32[8,128]{1,0:T(8,128)S(1)}, s32[8,128]{1,0:T(8,128)}, u32[]{:S(2)}) copy-start(s32[8,128]{1,0:T(8,128)} %get-tuple-element.10.table_ref) | copy-start | bytes 12292
  213.9 30.6 %all-to-all-start.1 = ((bf16[4,64,4096]{2,1,0:T(8,128)(2,1)}), bf16[4,64,4096]{2,1,0:T(8,128)(2,1)S(1)}, u32[]{:S(2)}, u32[]{:S(2)}) async-start(bf16[4,64,4096]{2,1,0:T(8,128)(2,1)} %get-tuple-element.14), calls=%async_computation.1 | async-start | bytes 4194304 | tf_op jit(solution)/shard_map/all_to_all | solution.py:393
